TPU v7x, 256 devices: a whole 4x4x8 slice. The times are simulated.
256 devices in a mesh: gx: 8 (over y, z_lo), gy: 4 (over z_hi), gz: 8 (over x, core).
Axes of the slice: x: 4, y: 4, z: 8 (z_hi: 4, z_lo: 2; z = z_hi * 2 + z_lo), core: 2. Of those that a mesh axis runs over, the one named last changes fastest.
Arguments:
- features: bfloat16 [64, 4, 8, 64, 128], P('gx', 'gy', 'gz'), may hold values from -6 to 6
- positions: bfloat16 [64, 4, 8, 3, 128], P('gx', 'gy', 'gz'), may hold values from 0 to 1
- counts: int32 [64, 4, 8], P('gx', 'gy', 'gz'), may hold values from 1 to 128, as said below
- old_cuts: int32 [9], replicated, may hold values from 0 to 32, as said below
- new_cuts: int32 [9], replicated, may hold values from 0 to 32, as said below
- radial_rates: float32 [2, 2], replicated, may hold values from 0.3 to 3
- conv_weight: bfloat16 [2, 64, 2, 64], replicated, may hold values from -0.5 to 0.5
- up_weight: bfloat16 [2, 256, 64], replicated, may hold values from -0.75 to 0.75
- up_bias: float32 [2, 256], replicated, may hold values from -3 to 3
- down_weight: bfloat16 [2, 64, 256], replicated, may hold values from -0.375 to 0.375
- down_bias: float32 [2, 64], replicated, may hold values from -2 to 2
Outputs:
- moved: bfloat16 [64, 4, 8, 64, 128], P('gx', 'gy', 'gz')
Inputs may be any that keep to these rules, and one draw needn't show every extreme that they name: `counts`: some bin of the first x layer holds exactly 128 particles. `old_cuts`: rising from 0 to 32; index k of gx holds the x layers from old_cuts[k] to old_cuts[k+1] - 1, from 2 to 8 of them; with three or more indices along gx one holds exactly 8. `new_cuts`: same form as old_cuts, and each cut differs from the one of old_cuts by -1, 0 or 1.
All inputs are finite; a program needn't handle non-finite values.
Results may differ from a plain program's by a relative error of at most 0.0058.
Values may be sent and summed in bfloat16 or wider, within the bound.
A program may use at most 128 MiB of HBM per device.

v0:
```python
import jax
import jax.numpy as jnp
from jax import lax
from jax.experimental import pallas as pl
from jax.experimental.pallas import tpu as pltpu
from jax.sharding import PartitionSpec as P

MESH = pl.DeviceIdType.MESH
BF = jnp.bfloat16
F32 = jnp.float32
EPSILON = 1e-05
LOG2E = 1.4426950408889634

N_GX, N_GY, N_GZ = 8, 4, 8
SLOT_CAP, OWN = 8, 4
F, J, HID = 64, 128, 256

COLUMN = 432
ROW = (352, 16, 80, 144, 208, 288)
TILE, TILE_ABOVE, TILE_BELOW = 0, 272, 416
PARCEL = 272

SHARE_FROM = {0: (0, 7), 1: (0, 6), -1: (1, 7), 2: (1, 4), -2: (3, 6), 3: (2, 2), -3: (5, 5)}
ENDS = (-1, 1)
CORNERS = ((-1, -1), (1, -1), (-1, 1), (1, 1))
PARTS = (((0, 272),), ((80, 128), (16, 64), (208, 64)))
PART_LAYERS = (((1, 2, 3, 4),), ((2, 3), (1,), (4,)))
INNER, HALO = (1, 2, 3, 4), (0, 5)
HOME = ((1, 2), (0, 1), (3, 1))


def name_copies():
    names = [("share", d) for d in SHARE_FROM]
    for phase in range(2):
        names += [("x", phase, dx) for dx in ENDS]
        names += [("xy", phase, dx, dy) for dx, dy in CORNERS]
        for part in range(len(PARTS[phase])):
            names += [("y", phase, dy, part) for dy in ENDS]
            names += [("z", phase, dz, y, part) for dz in ENDS for y in range(3)]
        names += [("zx", phase, dz, y) for dz in ENDS for y in range(3)]
    names += [("home", d, part) for d in SHARE_FROM for part in range(len(HOME))]
    return {name: number for number, name in enumerate(names)}


NUMBER = name_copies()


def snake(k):
    return k + ((k // 2) % 2) * (1 - 2 * (k % 2))


def gx_partners():
    met = {k: set() for k in range(N_GX)}
    for d, (low, high) in SHARE_FROM.items():
        for k in range(low, high + 1):
            met[k].add(snake(k + d))
            met[snake(k + d)].add(k)
    for s in range(N_GX - 1):
        met[snake(s)].add(snake(s + 1))
        met[snake(s + 1)].add(snake(s))
    return {j: sorted(k for k in met if j in met[k] and j != k) for j in range(N_GX)}


def within(value, low, high):
    return jnp.logical_and(value >= low, value <= high)


def either(conditions):
    result = conditions[0]
    for condition in conditions[1:]:
        result = jnp.logical_or(result, condition)
    return result


def kernel(
    features_in, positions_in, counts_in, old_cuts_in, new_cuts_in, rates_in, conv_w_in, up_w_in,
    up_b_in, down_w_in, down_b_in,
    out,
    features, positions, counts, old_cuts, new_cuts, rates, conv_w, up_w_read, up_b, down_w, down_b,
    up_w, masked, places, parcel, shared, tile, column0, column1, low_halo, near, own, acc, bias_up,
    bias_down, home, load_sem, send_sem, recv_sem,
):
    gx, gy, gz = lax.axis_index("gx"), lax.axis_index("gy"), lax.axis_index("gz")
    share = snake(gx)
    columns = (column0, column1)

    def keeper(s):
        return snake(jnp.clip(s, 0, N_GX - 1))

    def copy(name, source, target, device):
        return pltpu.make_async_remote_copy(
            src_ref=source, dst_ref=target, send_sem=send_sem.at[NUMBER[name]],
            recv_sem=recv_sem.at[NUMBER[name]], device_id=device, device_id_type=MESH,
        )

    def has(dx, dy, dz):
        ok = None
        for place, count, step in ((share, N_GX, dx), (gy, N_GY, dy), (gz, N_GZ, dz)):
            if step:
                here = place < count - 1 if step > 0 else place > 0
                ok = here if ok is None else jnp.logical_and(ok, here)
        return ok

    for cells in columns:

        @pl.when(share == 0)
        def _():
            for y in range(3):
                cells[1, y, ROW[0] : ROW[0] + 80, :] = jnp.zeros((80, J), BF)

        @pl.when(share == N_GX - 1)
        def _():
            for y in range(3):
                cells[1, y, TILE_ABOVE : TILE_ABOVE + 80, :] = jnp.zeros((80, J), BF)

        @pl.when(gy == 0)
        def _():
            cells[1, 0] = jnp.zeros((COLUMN, J), BF)

        @pl.when(gy == N_GY - 1)
        def _():
            cells[1, 2] = jnp.zeros((COLUMN, J), BF)

        @pl.when(gz == 0)
        def _():
            cells[0] = jnp.zeros((3, COLUMN, J), BF)

        @pl.when(gz == N_GZ - 1)
        def _():
            cells[2] = jnp.zeros((3, COLUMN, J), BF)

    partners = []
    for j, near_j in gx_partners().items():
        partners.append(((j, gy, gz), either([gx == k for k in near_j])))
    for dx, dy in CORNERS:
        partners.append(((keeper(share + dx), gy + dy, gz), has(dx, dy, 0)))
    for step in ENDS:
        partners.append(((gx, gy + step, gz), has(0, step, 0)))
        partners.append(((gx, gy, gz + step), has(0, 0, step)))
    barrier = pltpu.get_barrier_semaphore()
    peers = jnp.int32(0)
    for device, there in partners:
        peers = peers + jnp.where(there, 1, 0)

        @pl.when(there)
        def _():
            pl.semaphore_signal(barrier, inc=1, device_id=device, device_id_type=MESH)

    arguments = (
        (counts_in, counts), (old_cuts_in, old_cuts), (features_in, features),
        (positions_in, positions), (up_b_in, up_b), (down_b_in, down_b), (up_w_in, up_w_read),
        (conv_w_in, conv_w), (down_w_in, down_w), (rates_in, rates), (new_cuts_in, new_cuts),
    )
    loads = [
        pltpu.make_async_copy(source, target, load_sem.at[n])
        for n, (source, target) in enumerate(arguments)
    ]
    for load in loads:
        load.start()
    for load in loads[:4]:
        load.wait()

    particle = lax.broadcasted_iota(jnp.int32, (1, J), 1)
    for slot in range(SLOT_CAP):
        live = (particle < counts[slot]).astype(F32)
        masked[slot] = (features[slot].astype(F32) * live).astype(BF)
        for c in range(3):
            places[slot, c : c + 1, :] = positions[c].astype(F32)[slot : slot + 1, :]
        places[slot, 3:4, :] = live

    def share_sent(d):
        low, high = SHARE_FROM[d]
        return within(gx, low, high), keeper(gx + d)

    def share_came(d):
        low, high = SHARE_FROM[d]
        return jnp.logical_and(within(share - d, low, high), share - d != gx)

    def share_copy(d):
        return copy(
            ("share", d), parcel.at[d + 3], shared.at[d + 3], (share_sent(d)[1], gy, gz)
        )

    for d in SHARE_FROM:
        used, device = share_sent(d)

        @pl.when(used)
        def _():
            for t in range(OWN):
                slot = jnp.clip((gx + d) * OWN + t - old_cuts[gx], 0, SLOT_CAP - 1)
                parcel[d + 3, 16 + F * t : 16 + F * (t + 1), :] = masked[slot]
                tile[4 * t : 4 * t + 4, :] = places[slot, 0:4, :]
            parcel[d + 3, 0:16, :] = tile[...].astype(BF)

        @pl.when(jnp.logical_and(used, device == gx))
        def _():
            shared[d + 3] = parcel[d + 3]

    pl.semaphore_wait(barrier, peers)

    for d in SHARE_FROM:
        used, device = share_sent(d)
        pl.when(jnp.logical_and(used, device != gx))(lambda d=d: share_copy(d).start())
    for load in loads[4:]:
        load.wait()
    for phase in range(2):
        for half in range(2):
            row = up_b[phase : phase + 1, J * half : J * (half + 1)]
            bias_up[phase, J * half : J * (half + 1), :] = jnp.broadcast_to(row, (J, J)).T
        row = down_b[phase : phase + 1, :]
        row = jnp.concatenate([row, row], axis=1)
        bias_down[phase] = jnp.broadcast_to(row, (J, J)).T[:F]
        up_w[phase] = up_w_read[phase].astype(F32).T.astype(BF)

    for d in SHARE_FROM:
        pl.when(share_came(d))(lambda d=d: share_copy(d).wait_recv())

    for t in range(OWN):
        place = share * OWN + t
        holder = jnp.int32(0)
        for k in range(1, N_GX):
            holder = holder + jnp.where(old_cuts[k] <= place, 1, 0)
        came = jnp.clip(share - holder + 3, 0, 6)
        column0[1, 1, ROW[t + 1] : ROW[t + 1] + F, :] = shared[came, 16 + F * t : 16 + F * (t + 1), :]
        tile[4 * t : 4 * t + 4, :] = shared[came, 0:16, :].astype(F32)[4 * t : 4 * t + 4]
    column0[1, 1, 0:16, :] = tile[...].astype(BF)
    low_halo[0:F, :] = column0[1, 1, ROW[4] : ROW[4] + F, :]
    low_halo[F : F + 16, :] = tile[...].astype(BF)

    def x_copy(phase, dx, dy):
        cells, y = columns[phase], 1 - dy
        extra = 16 if phase == 0 else 0
        if dx == 1:
            source = low_halo if phase == 0 else cells.at[1, 1, pl.ds(ROW[4], F)]
            target = cells.at[1, y, pl.ds(ROW[0], F + extra)]
        else:
            source = cells.at[1, 1, pl.ds(ROW[1] - extra, F + extra)]
            target = cells.at[1, y, pl.ds(ROW[5] - extra, F + extra)]
        name = ("xy", phase, dx, dy) if dy else ("x", phase, dx)
        return copy(name, source, target, (keeper(share + dx), gy + dy, gz))

    def y_copy(phase, dy, part):
        cells, rows = columns[phase], pl.ds(*PARTS[phase][part])
        return copy(
            ("y", phase, dy, part), cells.at[1, 1, rows], cells.at[1, 1 - dy, rows],
            (gx, gy + dy, gz),
        )

    def z_copy(phase, dz, y, part):
        cells, rows = columns[phase], pl.ds(*PARTS[phase][part])
        return copy(
            ("z", phase, dz, y, part), cells.at[1, y, rows], cells.at[1 - dz, y, rows],
            (gx, gy, gz + dz),
        )

    def zx_copy(phase, dz, y):
        cells, rows = columns[phase], pl.ds(TILE_ABOVE, 160) if phase == 0 else pl.ds(ROW[5], 128)
        return copy(
            ("zx", phase, dz, y), cells.at[1, y, rows], cells.at[1 - dz, y, rows],
            (gx, gy, gz + dz),
        )

    def locate(z, y, inner):
        step = lax.broadcasted_iota(jnp.int32, (4, J), 0)
        if inner:
            rows = column0[z, y, TILE : TILE + 16, :].astype(F32)
            rows = {t + 1: rows[4 * t : 4 * t + 4] for t in range(OWN)}
        else:
            below = column0[z, y, TILE_BELOW : TILE_BELOW + 16, :].astype(F32)
            above = column0[z, y, TILE_ABOVE : TILE_ABOVE + 16, :].astype(F32)
            rows = {0: below[12:16], 5: above[0:4]}
        for l, row in rows.items():
            shift = jnp.where(step == 0, float(l), jnp.where(step == 1, y - 1.0, z - 1.0))
            near[z, y, l, 0:4, :] = row - shift

    begun = set()

    def convolve(phase, cells_of, layers, bins=range(OWN)):
        cells = columns[phase]
        scale = [rates[phase, m] * -LOG2E for m in range(2)]
        for b in bins:
            beside = [(z, y, l) for l in layers if b <= l <= b + 2 for z, y in cells_of]
            if not beside:
                continue
            if (phase, b) in begun:
                total = [acc[b, m] for m in range(2)]
            else:
                total = [jnp.zeros((J, F), F32) for m in range(2)]
                begun.add((phase, b))
            for g in range(0, len(beside), 2):
                h, kern = [], [[], []]
                for z, y, l in beside[g : g + 2]:
                    h.append(cells[z, y, ROW[l] : ROW[l] + F, :])
                    dist = None
                    for c in range(3):
                        r = own[b, c] - near[z, y, l, c : c + 1, :]
                        dist = r * r if dist is None else dist + r * r
                    for m in range(2):
                        kern[m].append(jnp.exp2(dist * scale[m]).astype(BF))
                h = jnp.concatenate(h, axis=1)
                for m in range(2):
                    total[m] = total[m] + lax.dot_general(
                        jnp.concatenate(kern[m], axis=1), h, (((1,), (1,)), ((), ())),
                        preferred_element_type=F32,
                    )
            for m in range(2):
                acc[b, m] = total[m]

    def update(phase, bins):
        gathered = [jnp.concatenate([acc[b, m] for b in bins], axis=0).astype(BF) for m in range(2)]
        mixed = None
        for m in range(2):
            term = lax.dot_general(
                conv_w[phase, :, m, :], gathered[m], (((1,), (1,)), ((), ())),
                preferred_element_type=F32,
            )
            mixed = term if mixed is None else mixed + term
        centred = mixed - jnp.mean(mixed, axis=0, keepdims=True)
        spread = jnp.mean(centred * centred, axis=0, keepdims=True)
        normed = (centred * lax.rsqrt(spread + EPSILON)).astype(BF)
        raised = jnp.dot(up_w[phase], normed, preferred_element_type=F32)
        raised = raised + jnp.concatenate([bias_up[phase]] * 2, axis=1)
        hidden = jax.nn.silu(raised).astype(BF)
        change = jnp.dot(down_w[phase], hidden, preferred_element_type=F32)
        change = change + jnp.concatenate([bias_down[phase]] * 2, axis=1)
        for n, b in enumerate(bins):
            before = columns[phase][1, 1, ROW[b + 1] : ROW[b + 1] + F, :].astype(F32)
            live = near[1, 1, b + 1, 3:4, :]
            after = ((before + change[:, J * n : J * (n + 1)]) * live).astype(BF)
            if phase == 0:
                column1[1, 1, ROW[b + 1] : ROW[b + 1] + F, :] = after
            else:
                home[share * OWN + b] = after

    def home_copy(d, part):
        first, count = HOME[part]
        rows = home.at[pl.ds(share * OWN + first, count)]
        return copy(("home", d, part), rows, rows, (share - d, gy, gz))

    def start_z(phase, parts):
        for dz in ENDS:

            @pl.when(has(0, 0, dz))
            def _():
                for part in parts:
                    z_copy(phase, dz, 1, part).start()

    def start_y(phase, parts):
        for dy in ENDS:

            @pl.when(has(0, dy, 0))
            def _():
                for part in parts:
                    y_copy(phase, dy, part).start()

    def start_x(phase):
        for dx in ENDS:
            pl.when(has(dx, 0, 0))(lambda dx=dx: x_copy(phase, dx, 0).start())

    def start_corners(phase):
        for dx, dy in CORNERS:
            pl.when(has(dx, dy, 0))(lambda dx=dx, dy=dy: x_copy(phase, dx, dy).start())

    def start_home(parts):
        for part in parts:
            for d in SHARE_FROM:
                pl.when(share_came(d))(lambda d=d, p=part: home_copy(d, p).start())

    def forward(phase, y, part):
        dy = 1 - y
        pl.when(has(0, -dy, 0))(lambda: y_copy(phase, dy, part).wait_recv())
        for dz in ENDS:
            pl.when(has(0, 0, dz))(lambda dz=dz: z_copy(phase, dz, y, part).start())

    def forward_halo(phase, y):
        dy = 1 - y
        for dx in ENDS:
            pl.when(has(-dx, -dy, 0))(lambda dx=dx: x_copy(phase, dx, dy).wait_recv())
        for dz in ENDS:
            pl.when(has(0, 0, dz))(lambda dz=dz: zx_copy(phase, dz, y).start())

    def receive_z(phase, y, part):
        for dz in ENDS:
            pl.when(has(0, 0, -dz))(lambda dz=dz: z_copy(phase, dz, y, part).wait_recv())

    def receive_zx(phase, y):
        for dz in ENDS:
            pl.when(has(0, 0, -dz))(lambda dz=dz: zx_copy(phase, dz, y).wait_recv())

    def finish_share():
        for d in SHARE_FROM:
            used, device = share_sent(d)
            pl.when(jnp.logical_and(used, device != gx))(lambda d=d: share_copy(d).wait_send())

    def finish_home():
        for d in SHARE_FROM:

            @pl.when(share_came(d))
            def _():
                for part in range(len(HOME)):
                    home_copy(d, part).wait_send()

    def finish(phase):
        parts = range(len(PARTS[phase]))
        for dx in ENDS:
            for dy in (-1, 0, 1):
                pl.when(has(dx, dy, 0))(lambda dx=dx, dy=dy: x_copy(phase, dx, dy).wait_send())
        for dy in ENDS:

            @pl.when(has(0, dy, 0))
            def _():
                for part in parts:
                    y_copy(phase, dy, part).wait_send()

        for dz in ENDS:

            @pl.when(has(0, 0, dz))
            def _():
                for y in range(3):
                    zx_copy(phase, dz, y).wait_send()
                    for part in parts:
                        z_copy(phase, dz, y, part).wait_send()

    def find(phase, cells_of, inner):
        if phase == 0:
            for z, y in cells_of:
                locate(z, y, inner)

    def layer(phase):
        parts = range(len(PARTS[phase]))
        sides, beside = [(0, 1), (2, 1)], [(1, 0), (1, 2)]
        fresh = parts if phase == 0 else parts[1:]
        start_x(phase)
        start_y(phase, fresh)
        start_corners(phase)
        start_z(phase, fresh)
        if phase == 0:
            for b in range(OWN):
                for c in range(3):
                    row = tile[4 * b + c : 4 * b + c + 1, :]
                    row = row - float(b + 1) if c == 0 else row
                    own[b, c] = jnp.broadcast_to(row, (J, J)).T
        find(phase, [(1, 1)], True)
        convolve(phase, [(1, 1)], INNER)
        if phase == 1:
            finish_share()
            finish(0)
            forward(phase, 0, 0)
            forward(phase, 2, 0)
        forward_halo(phase, 1)
        find(phase, [(1, 1)], False)
        convolve(phase, [(1, 1)], HALO)
        corners = [[(0, 0), (2, 0)], [(0, 2), (2, 2)]]
        if phase == 0:
            for part in parts:
                forward(phase, 0, part)
                forward(phase, 2, part)
            for part in parts:
                receive_z(phase, 1, part)
                if part == 0:
                    find(phase, sides, True)
                convolve(phase, sides, PART_LAYERS[phase][part])
            find(phase, beside, True)
            convolve(phase, beside, INNER)
            forward_halo(phase, 0)
            forward_halo(phase, 2)
        else:
            receive_z(phase, 1, 0)
            convolve(phase, sides, PART_LAYERS[phase][0])
            convolve(phase, beside, PART_LAYERS[phase][0])
            for part in parts[1:]:
                forward(phase, 0, part)
                forward(phase, 2, part)
            for part in parts[1:]:
                receive_z(phase, 1, part)
            convolve(phase, sides, (1, 4))
            convolve(phase, beside, (1, 4))
            forward_halo(phase, 0)
            forward_halo(phase, 2)
        for y in (0, 2):
            receive_z(phase, y, 0)
            find(phase, corners[y // 2], True)
            convolve(phase, corners[y // 2], PART_LAYERS[phase][0])
        receive_zx(phase, 1)
        find(phase, sides, False)
        convolve(phase, sides, HALO)
        find(phase, beside, False)
        convolve(phase, beside, HALO)
        rest = [l for part in parts[1:] for l in PART_LAYERS[phase][part]]
        for y in (0, 2):
            for part in parts[1:]:
                receive_z(phase, y, part)
            convolve(phase, corners[y // 2], rest, (1, 2))
        update(phase, (1, 2))
        if phase == 0:
            start_y(1, (0,))
            start_z(1, (0,))
        else:
            start_home((0,))
        for y in (0, 2):
            convolve(phase, corners[y // 2], rest, (0, 3))
        for y in (0, 2):
            receive_zx(phase, y)
            find(phase, corners[y // 2], False)
            convolve(phase, corners[y // 2], HALO)
        update(phase, (0, 3))

    layer(0)
    layer(1)
    start_home((1, 2))
    finish(1)
    finish_home()

    for d in SHARE_FROM:
        used, device = share_sent(d)

        @pl.when(jnp.logical_and(used, device != gx))
        def _():
            for part, (first, count) in enumerate(HOME):
                rows = home.at[pl.ds((gx + d) * OWN + first, count)]
                copy(("home", d, part), rows, rows, (device, gy, gz)).wait_recv()

    held = new_cuts[gx + 1] - new_cuts[gx]
    for slot in range(SLOT_CAP):
        place = jnp.clip(new_cuts[gx] + slot, 0, N_GX * OWN - 1)
        keep = jnp.broadcast_to(held, (F, J)) > slot
        out[slot] = jnp.where(keep, home[place].astype(F32), 0.0).astype(BF)


def local(
    features, positions, counts, old_cuts, new_cuts, radial_rates, conv_weight, up_weight, up_bias,
    down_weight, down_bias,
):
    result = pl.pallas_call(
        kernel,
        out_shape=pltpu.VMEM((SLOT_CAP, F, J), BF),
        in_specs=[pl.BlockSpec(memory_space=pl.ANY)] * 11,
        out_specs=pl.BlockSpec(memory_space=pltpu.VMEM),
        scratch_shapes=[
            pltpu.VMEM((SLOT_CAP, F, J), BF),
            pltpu.VMEM((3, SLOT_CAP, J), BF),
            pltpu.SMEM((SLOT_CAP,), jnp.int32),
            pltpu.SMEM((N_GX + 1,), jnp.int32),
            pltpu.SMEM((N_GX + 1,), jnp.int32),
            pltpu.SMEM((2, 2), F32),
            pltpu.VMEM((2, F, 2, F), BF),
            pltpu.VMEM((2, F, HID), BF),
            pltpu.VMEM((2, HID), F32),
            pltpu.VMEM((2, F, HID), BF),
            pltpu.VMEM((2, F), F32),
            pltpu.VMEM((2, HID, F), BF),
            pltpu.VMEM((SLOT_CAP, F, J), BF),
            pltpu.VMEM((SLOT_CAP, 8, J), F32),
            pltpu.VMEM((7, PARCEL, J), BF),
            pltpu.VMEM((7, PARCEL, J), BF),
            pltpu.VMEM((16, J), F32),
            pltpu.VMEM((3, 3, COLUMN, J), BF),
            pltpu.VMEM((3, 3, COLUMN, J), BF),
            pltpu.VMEM((80, J), BF),
            pltpu.VMEM((3, 3, OWN + 2, 8, J), F32),
            pltpu.VMEM((OWN, 3, J, J), F32),
            pltpu.VMEM((OWN, 2, J, F), F32),
            pltpu.VMEM((2, HID, J), F32),
            pltpu.VMEM((2, F, J), F32),
            pltpu.VMEM((N_GX * OWN, F, J), BF),
            pltpu.SemaphoreType.DMA((11,)),
            pltpu.SemaphoreType.DMA((len(NUMBER),)),
            pltpu.SemaphoreType.DMA((len(NUMBER),)),
        ],
        compiler_params=pltpu.CompilerParams(
            collective_id=0, has_side_effects=True, vmem_limit_bytes=60 * 2**20
        ),
    )(
        features.reshape(SLOT_CAP, F, J),
        positions.transpose(1, 2, 3, 0, 4).reshape(3, SLOT_CAP, J),
        counts.reshape(SLOT_CAP),
        old_cuts,
        new_cuts,
        radial_rates,
        conv_weight,
        up_weight.transpose(0, 2, 1),
        up_bias,
        down_weight,
        down_bias,
    )
    return result.reshape(SLOT_CAP, 1, 1, F, J)


def solution(mesh):
    grid = P("gx", "gy", "gz")
    return jax.shard_map(
        local,
        mesh=mesh,
        in_specs=(grid, grid, grid) + (P(),) * 8,
        out_specs=grid,
        check_vma=False,
    )
```

profile of v0, /device:TPU:32, one launch (start us, length us, event | category | flops | bytes accessed | tf_op | source)
XLA Modules:
  0.0 41.4 jit_solution(12311252464750060623)
XLA Ops:
  0.0 40.7 %shard_map.109 = bf16[8,64,128]{2,1,0:T(8,128)(2,1)S(1)} custom-call(bf16[8,64,128]{2,1,0:T(8,128)(2,1)} %bitcast.10, bf16[3,8,128]{2,1,0:T(8,128)(2,1)} %bitcast.12, s32[8]{0:T(128)} %bitcast.13, s32[9]{0:T(128)} %old_cuts_in.1, s32[9]{0:T(128)} %new_cuts_in.1, f32[2,2]{1,0:T(2,128)} %rates_in.1, bf16[2,64,2,64]{3,2,1,0:T(2,128)(2,1)} %conv_w_in.1, ...), custom_call_target="tpu_custom_call" | custom-call | tf_op jit(solution)/shard_map/pallas_call | solution.py:534
  40.7 0.7 %copy.14 = bf16[8,1,1,64,128]{4,3,2,1,0:T(8,128)(2,1)} copy(bf16[8,1,1,64,128]{4,3,2,1,0:T(8,128)(2,1)S(1)} %bitcast.9) | data formatting | bytes 262144
where the time goes:
time: 41.5 us; the launch traced here: 41.4 us
  Pallas kernels  40.7 us (98%)
  local copies, waits for them, and re-layouts  0.66 us (2%)
    pallas_call x1, Pallas kernels, local(): pl.pallas_call(kernel, out_shape=pltpu.VMEM((SLOT_CAP, F, J), BF), in_spe...  40.7 us

commit v1 on v0

--- a/solution.py
+++ b/solution.py
@@ -443,8 +443,6 @@
         find(phase, [(1, 1)], True)
         convolve(phase, [(1, 1)], INNER)
         if phase == 1:
-            finish_share()
-            finish(0)
             forward(phase, 0, 0)
             forward(phase, 2, 0)
         forward_halo(phase, 1)
@@ -508,6 +506,8 @@
     layer(0)
     layer(1)
     start_home((1, 2))
+    finish_share()
+    finish(0)
     finish(1)
     finish_home()
 

time: 41.5 us -> 41.5 us (level)
  no operation moved by 1% of the time
where the time goes in v1:
time: 41.5 us; the launch traced here: 41.4 us
  Pallas kernels  40.7 us (98%)
  local copies, waits for them, and re-layouts  0.66 us (2%)
    pallas_call x1, Pallas kernels, local(): pl.pallas_call(kernel, out_shape=pltpu.VMEM((SLOT_CAP, F, J), BF), in_spe...  40.7 us

profile of v1, /device:TPU:32, one launch (start us, length us, event | category | flops | bytes accessed | tf_op | source)
XLA Modules:
  0.0 41.4 jit_solution(13111530263248575758)
XLA Ops:
  0.0 40.7 %shard_map.109 = bf16[8,64,128]{2,1,0:T(8,128)(2,1)S(1)} custom-call(bf16[8,64,128]{2,1,0:T(8,128)(2,1)} %bitcast.10, bf16[3,8,128]{2,1,0:T(8,128)(2,1)} %bitcast.12, s32[8]{0:T(128)} %bitcast.13, s32[9]{0:T(128)} %old_cuts_in.1, s32[9]{0:T(128)} %new_cuts_in.1, f32[2,2]{1,0:T(2,128)} %rates_in.1, bf16[2,64,2,64]{3,2,1,0:T(2,128)(2,1)} %conv_w_in.1, ...), custom_call_target="tpu_custom_call" | custom-call | tf_op jit(solution)/shard_map/pallas_call | solution.py:534
  40.7 0.7 %copy.14 = bf16[8,1,1,64,128]{4,3,2,1,0:T(8,128)(2,1)} copy(bf16[8,1,1,64,128]{4,3,2,1,0:T(8,128)(2,1)S(1)} %bitcast.9) | data formatting | bytes 262144
